TPU v7x, 768 devices: a whole 4x8x12 slice. The times are simulated.
768 devices in a mesh: dp: 12 (over z), mp: 64 (over x, y, core).
Axes of the slice: x: 4, y: 8, z: 12, core: 2. Of those that a mesh axis runs over, the one named last changes fastest.
Arguments:
- patches: bfloat16 [2304, 6144], P('dp', 'mp'), may hold values from -6 to 6
- table: float32 [256, 6144], P(None, 'mp'), may hold values from -6 to 6
- row_anchor: int32 [2304, 2], P('dp'), may hold values from 0 to 14
- row_frac: float32 [2304, 2], P('dp'), may hold values from 0 to 1
- group_rows: int32 [12], replicated, may hold values from 8 to 192, as said below
- up_weight: bfloat16 [6144, 24576], P(None, 'mp'), may hold values from -0.078125 to 0.078125
- down_weight: bfloat16 [24576, 6144], P('mp'), may hold values from -0.0390625 to 0.0390625
- cotangent: bfloat16 [2304, 6144], P('dp', 'mp'), may hold values from -6 to 6
Outputs:
- grad_patches: float32 [2304, 6144], P('dp', 'mp')
- grad_table: float32 [256, 6144], P(None, 'mp')
Inputs may be any that keep to these rules, and one draw needn't show every extreme that they name: `group_rows`: the entries sum to 768; one group holds exactly 192 tokens.
All inputs are finite; a program needn't handle non-finite values.
Results may differ from a plain program's by a relative error of at most 0.0026.
Values may be sent and summed in bfloat16 or wider, within the bound.
A program may use at most 64 MiB of HBM per device.

v0:
```python
import jax
import jax.numpy as jnp
from jax import lax
from jax.sharding import PartitionSpec as P

GRID = 16


def corners(row_anchor, row_frac):
    top = row_anchor[:, 0] * GRID + row_anchor[:, 1]
    cells = jnp.stack([top, top + 1, top + GRID, top + GRID + 1], axis=1)
    fy = row_frac[:, 0]
    fx = row_frac[:, 1]
    shares = jnp.stack([(1.0 - fy) * (1.0 - fx), (1.0 - fy) * fx, fy * (1.0 - fx), fy * fx], axis=1)
    return (cells, shares)


def gelu_slope(pre):
    normal_cdf = 0.5 * (1.0 + lax.erf(pre * 0.7071067811865476))
    density = jnp.exp(-0.5 * pre * pre) * 0.3989422804014327
    return normal_cdf + pre * density


def branch_grad(rows_in, rows_cot, up_weight, down_weight):
    in_piece = lax.all_gather(rows_in, "mp", axis=1, tiled=True)
    cot_piece = lax.all_gather(rows_cot, "mp", axis=1, tiled=True)
    pre_sum = jnp.dot(in_piece, up_weight, preferred_element_type=jnp.float32)
    back_sum = lax.dot_general(
        cot_piece, down_weight, (((1,), (1,)), ((), ())), preferred_element_type=jnp.float32
    )
    grad_pre = (back_sum * gelu_slope(pre_sum)).astype(jnp.bfloat16)
    term = lax.dot_general(
        grad_pre, up_weight, (((1,), (1,)), ((), ())), preferred_element_type=jnp.float32
    )
    branch = lax.psum_scatter(term, "mp", scatter_dimension=1, tiled=True)
    return rows_cot.astype(jnp.float32) + branch


def shards(patches, table, row_anchor, row_frac, group_rows, up_weight, down_weight, cotangent):
    slots = patches.shape[0]
    cells_count = table.shape[0]
    groups = lax.axis_size("dp")
    group_id = lax.axis_index("dp")
    group_ids = jnp.arange(groups, dtype=jnp.int32)
    own_count = jnp.sum(jnp.where(group_ids == group_id, group_rows, 0))
    local_ids = jnp.arange(slots, dtype=jnp.int32)
    live_rows = local_ids < own_count
    cells, shares = corners(row_anchor, row_frac)
    cell_ids = jnp.arange(cells_count, dtype=jnp.int32)
    weights_matrix = jnp.sum(
        jnp.where(cells[:, :, None] == cell_ids[None, None, :], shares[:, :, None], 0.0), axis=1
    )
    interp = jnp.dot(
        weights_matrix, table, precision=lax.Precision.HIGHEST, preferred_element_type=jnp.float32
    )
    inputs = (patches.astype(jnp.float32) + interp).astype(jnp.bfloat16)
    grad_rows = branch_grad(inputs, cotangent, up_weight, down_weight)
    grad_patches = jnp.where(live_rows[:, None], grad_rows, 0.0)
    partial_table = lax.dot_general(
        weights_matrix,
        grad_patches,
        (((0,), (0,)), ((), ())),
        precision=lax.Precision.HIGHEST,
        preferred_element_type=jnp.float32,
    )
    grad_table = lax.psum(partial_table, "dp")
    return (grad_patches, grad_table)


def solution(mesh):
    in_specs = (
        P("dp", "mp"),
        P(None, "mp"),
        P("dp", None),
        P("dp", None),
        P(),
        P(None, "mp"),
        P("mp", None),
        P("dp", "mp"),
    )
    out_specs = (P("dp", "mp"), P(None, "mp"))
    return jax.shard_map(shards, mesh=mesh, in_specs=in_specs, out_specs=out_specs, check_vma=False)
```

profile of v0, /device:TPU:1, one launch (start us, length us, event | category | flops | bytes accessed | tf_op | source)
XLA Modules:
  0.0 486.6 jit_solution(4950506560865899774)
XLA Ops:
  7.2 0.0 copy-start
  7.2 0.0 all-gather.5.cloned.1.call-start
  7.2 0.8 subtract_multiply_fusion.1
  8.0 0.8 broadcast_add_fusion.1
  8.8 0.3 select_reduce_fusion
  9.1 0.0 copy-done
  9.1 1.1 fusion.1
  10.2 0.7 copy.17
  10.9 0.0 all-gather.5.cloned.1.call-update
  11.0 0.0 all-gather.3.cloned.1.call-start
  11.0 1.5 copy.16
  12.5 0.0 all-gather.3.cloned.1.call-update
  12.5 0.0 reduce-scatter.4.cloned.1.call-start
  12.6 96.9 %all-gather.5.cloned.1.call-done = bf16[192,6144]{0,1:T(8,128)(2,1)} async-done(((bf16[192,96]{0,1:T(8,128)(2,1)}), bf16[192,6144]{0,1:T(8,128)(2,1)}) %all-gather.5.cloned.1.call-update) | async-done | bytes 2359312 | tf_op jit(solution)/shard_map/all_gather | solution.py:25
  109.5 4.7 fusion.22
  114.2 86.7 %all-gather.3.cloned.1.call-done = bf16[192,6144]{0,1:T(8,128)(2,1)} async-done(((bf16[192,96]{0,1:T(8,128)(2,1)}), bf16[192,6144]{0,1:T(8,128)(2,1)}) %all-gather.3.cloned.1.call-update) | async-done | bytes 2359312 | tf_op jit(solution)/shard_map/all_gather | solution.py:26
  200.9 11.2 %convolution_bitcast_fusion = f32[6144,192]{1,0:T(8,128)} fusion(bf16[6144,384]{1,0:T(8,128)(2,1)} %param.13, bf16[192,6144]{0,1:T(8,128)(2,1)} %all-gather.3.cloned.1.call-done, bf16[384,6144]{1,0:T(8,128)(2,1)} %param.14, f32[192,384]{1,0:T(8,128)S(1)} %fusion.22), kind=kOutput, calls=%fused_computation | convolution fusion | flops 1812676608 | bytes 16809984
  212.1 0.0 copy-start.3
  212.1 0.0 copy-start.2
  212.1 0.0 reduce-scatter.4.cloned.1.call-update
  212.1 0.0 all-reduce.2.cloned.1.call-start
  212.2 0.6 copy-done.3
  212.8 0.6 fusion.16
  213.4 0.6 iota_compare_fusion.1
  214.0 154.7 %reduce-scatter.4.cloned.1.call-done = f32[96,192]{1,0:T(8,128)} async-done(((f32[6144,192]{1,0:T(8,128)}), f32[96,192]{1,0:T(8,128)}) %reduce-scatter.4.cloned.1.call-update) | async-done | bytes 73744
  368.7 1.0 copy.19
  369.7 0.0 copy-done.2
  369.7 0.1 add_select_fusion
  369.8 0.0 copy-start.1
  369.8 1.0 fusion.23
  370.9 0.0 all-reduce.2.cloned.1.call-update
  370.9 107.7 %all-reduce.2.cloned.1.call-done = f32[256,96]{0,1:T(8,128)} async-done(((f32[256,96]{0,1:T(8,128)}), f32[256,96]{0,1:T(8,128)}) %all-reduce.2.cloned.1.call-update) | async-done | bytes 98320 | tf_op jit(solution)/shard_map/psum | solution.py:66
  478.6 1.5 copy.21
  480.1 0.0 copy-done.1
  (3 shorter events, 0.0 us)
Async XLA Ops:
  7.2 1.9 copy-start
  7.2 102.3 %all-gather.5.cloned.1.call-start = ((), (), s32[]{:S(2)}) async-start(), calls=%async_computation.2 | async-start | bytes 3194880 | tf_op jit(solution)/shard_map/all_gather | solution.py:25
  11.0 189.9 %all-gather.3.cloned.1.call-start = ((), (), s32[]{:S(2)}) async-start(), calls=%async_computation.1 | async-start | bytes 3194880 | tf_op jit(solution)/shard_map/all_gather | solution.py:26
  12.5 356.2 %reduce-scatter.4.cloned.1.call-start = ((), (), s32[]{:S(2)}) async-start(), calls=%async_computation.4 | async-start | bytes 6389760
  212.1 0.7 copy-start.3
  212.1 157.6 %copy-start.2 = (bf16[192,96]{1,0:T(8,128)(2,1)S(1)}, bf16[192,96]{1,0:T(8,128)(2,1)}, u32[]{:S(2)}) copy-start(bf16[192,96]{1,0:T(8,128)(2,1)} %param.15) | copy-start | bytes 110596
  212.1 266.4 %all-reduce.2.cloned.1.call-start = ((), (), s32[]{:S(2)}) async-start(), calls=%async_computation.3 | async-start | bytes 196608 | tf_op jit(solution)/shard_map/psum | solution.py:66
  369.8 110.3 %copy-start.1 = (f32[192,96]{1,0:T(8,128)}, f32[192,96]{1,0:T(8,128)S(1)}, u32[]{:S(2)}) copy-start(f32[192,96]{1,0:T(8,128)S(1)} %add_select_fusion) | copy-start | bytes 221188
Sparse Core Ops, SparseCore 0:
  12.5 96.9 all-gather.4
  114.0 86.8 all-gather.2
  212.2 156.4 reduce-scatter.3
  371.6 106.9 all-reduce.1
where the time goes:
time: 494 us; the launch traced here: 487 us
  waiting for transfers between devices  446 us (90%)
  matrix products  18.1 us (4%)
  between operations  13.9 us (3%)
  local copies, waits for them, and re-layouts  5.35 us (1%)
    unnamed x5, waiting for transfers between devices  155 us
    psum x1, waiting for transfers between devices, shards(): grad_table = lax.psum(partial_table, 'dp')  108 us
    all_gather x1, waiting for transfers between devices, branch_grad(): in_piece = lax.all_gather(rows_in, 'mp', axis=1, tiled=True)  96.9 us
    all_gather x1, waiting for transfers between devices, branch_grad(): cot_piece = lax.all_gather(rows_cot, 'mp', axis=1, tiled=True)  86.7 us
    unnamed x1, matrix products  11.2 us
  transfers between devices with their start and end apart: 4, of which 4 were waited for; matrix products, arithmetic and copies ran while one was open for 2% of the time, Pallas kernels for 0%

commit v1 on v0

v1 whole, which is shorter than its diff:
```python
import jax
import jax.numpy as jnp
from jax import lax
from jax.experimental import pallas as pl
from jax.experimental.pallas import tpu as pltpu
from jax.sharding import PartitionSpec as P

MESH = pl.DeviceIdType.MESH
F32, BF16 = jnp.float32, jnp.bfloat16
GRID, CELLS, D, FF = 16, 256, 6144, 24576
NZ, NX, NY, NC = 12, 4, 8, 2
NMP = NX * NY * NC
CAP, BAL, TOKENS = 192, 64, 768
FEAT, HID = D // NMP, FF // NMP
PACK = CAP // NZ
HALF = FEAT // 2
BLOCK = NY * NC * FEAT
NN = (((1,), (0,)), ((), ()))
NT = (((1,), (1,)), ((), ()))
TN = (((0,), (0,)), ((), ()))


def dot(a, b, dims=NN):
    return lax.dot_general(a, b, dims, preferred_element_type=F32)


def iota(shape, dim):
    return lax.broadcasted_iota(jnp.int32, shape, dim)


def split2(v):
    high = v.astype(BF16)
    return high, (v - high.astype(F32)).astype(BF16)


def corner_weights(meta, first, rows):
    col = lambda k: meta[:, first + k : first + k + 1]
    a, b = col(0), col(1)
    p = (col(4) + col(3)) + col(2)
    q = (col(7) + col(6)) + col(5)
    cell = iota((rows, CELLS), 1)
    ca, cb = (cell >> 4).astype(F32), (cell & 15).astype(F32)
    wa = jnp.where(ca == a, 1.0 - p, jnp.where(ca == a + 1.0, p, 0.0))
    wb = jnp.where(cb == b, 1.0 - q, jnp.where(cb == b + 1.0, q, 0.0))
    return wa * wb


def gelu_slope(pre):
    cdf = 0.5 * (1.0 + lax.erf(pre * 0.7071067811865476))
    return cdf + pre * (jnp.exp(-0.5 * pre * pre) * 0.3989422804014327)


def kernel(
    rows_ref, patches_ref, cot_ref, table_ref, anchor_ref, frac_ref, up_hbm, down_hbm,
    gp_ref, gt_ref,
    up, down, msg, zin, cm, cmr, xt, term, sb, sr, xb, xr, yb, yr, gb, gr, own_ref,
    wsem, zs, zr, cs, cr, gys, gyr, gxs, gxr, gss, gsr, rss, rsr, rxs, rxr, rys, ryr, gzs, gzr,
):
    z, i = lax.axis_index("dp"), lax.axis_index("mp")
    x, y, c = i // (NY * NC), (i // NC) % NY, i % NC

    def device(zz, xx, yy, cc):
        return {"dp": zz, "mp": (xx * NY + yy) * NC + cc}

    zpeer = lambda o: lax.rem(z + o, NZ)
    xpeer = lambda o: lax.rem(x + o, NX)
    ypeer = lambda o: lax.rem(y + o, NY)
    sibling = device(z, x, y, 1 - c)
    sent = []

    def send(src, dst, ssem, rsem, dev):
        copy = pltpu.make_async_remote_copy(
            src_ref=src, dst_ref=dst, send_sem=ssem, recv_sem=rsem, device_id=dev, device_id_type=MESH
        )
        copy.start()
        sent.append(copy)
        return copy

    load_up = pltpu.make_async_copy(up_hbm, up, wsem.at[0])
    load_down = pltpu.make_async_copy(down_hbm, down, wsem.at[1])
    load_up.start()
    load_down.start()

    barrier = pltpu.get_barrier_semaphore()
    peers = [device(zpeer(o), x, y, c) for o in (6, 5, 7, 4, 8, 3, 9, 2, 10, 1, 11)]
    peers += [device(z, x, ypeer(o), c) for o in (4, 3, 5, 2, 6, 1, 7)]
    peers += [device(z, xpeer(o), y, c) for o in (2, 1, 3)] + [sibling]
    for dev in peers:
        pl.semaphore_signal(barrier, inc=1, device_id=dev, device_id_type=MESH)

    starts, count = [], jnp.int32(0)
    for g in range(NZ):
        starts.append(count)
        count = count + rows_ref[g]
    off = jnp.int32(0)
    for g in range(NZ):
        off = jnp.where(z == g, starts[g], off)
    own_rows = rows_ref[z]

    rho = iota((CAP, CAP), 0)
    turn = (rho >> 4) - lax.rem(off, NZ)
    slot = jnp.where(turn < 0, turn + NZ, turn) + NZ * (rho & (PACK - 1))
    perm = jnp.where(iota((CAP, CAP), 1) == slot, 1.0, 0.0).astype(BF16)

    a, b = anchor_ref[0:1, :].astype(F32), anchor_ref[1:2, :].astype(F32)
    parts = [a, b]
    for k in range(2):
        v = frac_ref[k : k + 1, :]
        for _ in range(3):
            part = v.astype(BF16).astype(F32)
            parts.append(part)
            v = v - part
    line = iota((128 - FEAT, CAP), 0)
    meta = jnp.zeros((128 - FEAT, CAP), F32)
    for k, part in enumerate(parts):
        meta = jnp.where(line == k, part, meta)
    meta = jnp.concatenate([jnp.zeros((FEAT, CAP), BF16), meta.astype(BF16)], axis=0)
    meta_rows = dot(perm, meta, NT)

    w_hi, w_lo = split2(corner_weights(meta_rows, FEAT, CAP))
    t_hi, t_lo = split2(table_ref[...])
    interp = dot(w_hi, t_hi, NT) + (dot(w_hi, t_lo, NT) + dot(w_lo, t_hi, NT))
    inputs = (dot(perm, patches_ref[...]) + interp).astype(BF16)
    msg[:, :, 0:128] = jnp.zeros((NZ, PACK, 128), BF16)
    msg[:, :, 0:FEAT] = inputs.reshape(NZ, PACK, FEAT)
    msg[:, :, 128:256] = meta_rows.astype(BF16).reshape(NZ, PACK, 128)
    msg[:, :, 128 : 128 + FEAT] = dot(perm, cot_ref[...]).astype(BF16).reshape(NZ, PACK, FEAT)

    pl.semaphore_wait(barrier, len(peers))

    z_order = (6, 5, 7, 4, 8, 3, 9, 2, 10, 1, 11)
    zc = [
        send(msg.at[zpeer(o)], zin.at[z], zs.at[o], zr.at[o], device(zpeer(o), x, y, c))
        for o in z_order
    ]
    zin[z] = msg[z]

    lane = iota((1, CAP), 1)
    group, j = lane >> 4, lane & (PACK - 1)
    place = jnp.zeros((1, CAP), jnp.int32)
    for g in range(NZ):
        o12, q12 = lax.rem(starts[g], NZ), lax.div(starts[g], NZ)
        turn = z - o12
        s = jnp.where(turn < 0, turn + NZ, turn) + NZ * j
        k = q12 + j + jnp.where(turn < 0, 1, 0)
        place = jnp.where(group == g, jnp.where(s < rows_ref[g], k, -1), place)
    compact = jnp.where(iota((BAL, CAP), 0) == place, 1.0, 0.0).astype(BF16)

    for copy in zc:
        copy.wait_recv()
    rows = dot(compact, zin[...].reshape(CAP, 256))
    both = jnp.concatenate([rows[:, :128], rows[:, 128:]], axis=0)
    xt[x, y, c] = both.T[:FEAT].astype(BF16)

    gy = [
        send(xt.at[x, y, c], xt.at[x, y, c], gys.at[o], gyr.at[o], device(z, x, ypeer(o), c))
        for o in (4, 3, 5, 2, 6, 1, 7)
    ]
    cm[...] = rows[:, 128:].astype(BF16)
    cmr[z] = cm[...]
    for copy in gy:
        copy.wait_recv()
    gx = {
        o: send(xt.at[x, :, c], xt.at[x, :, c], gxs.at[o], gxr.at[o], device(z, xpeer(o), y, c))
        for o in (2, 1, 3)
    }
    gs = {0: send(xt.at[x, :, c], xt.at[x, :, c], gss.at[0], gsr.at[0], sibling)}
    cz = [
        send(cm, cmr.at[z], cs.at[o], cr.at[o], device(zpeer(o), x, y, c)) for o in z_order
    ]

    load_up.wait()
    load_down.wait()

    def products(b):
        block = xt[b].reshape(BLOCK, 128)
        at = pl.multiple_of(b * BLOCK, BLOCK)
        return dot(block, up[pl.ds(at, BLOCK), :], TN), dot(down[:, pl.ds(at, BLOCK)], block)

    gs[0].wait_recv()
    pre, back = products(x)
    for o in (1, 3, 2):
        gx[o].wait_recv()
        b = xpeer(NX - o)
        gs[o] = send(xt.at[b, :, c], xt.at[b, :, c], gss.at[o], gsr.at[o], sibling)
    for o in (1, 3, 2):
        gs[o].wait_recv()
        more = products(xpeer(NX - o))
        pre, back = pre + more[0], back + more[1]

    low = iota((HID, 128), 1) < BAL
    grad = pltpu.roll(back, BAL, 1) * gelu_slope(pre.T)
    grad = jnp.where(low, grad, 0.0)
    pair = jnp.concatenate([grad, pltpu.roll(grad, BAL, 1)], axis=0).astype(BF16)

    rs = {}
    for o in (2, 1, 3, 0):
        b = xpeer(o)
        weights = up[pl.ds(pl.multiple_of(b * BLOCK, BLOCK), BLOCK), :]
        weights = weights.reshape(NY * NC, 2, HALF, HID)
        weights = jnp.concatenate([weights[:, 0], weights[:, 1]], axis=2)
        part = dot(weights.reshape(NY * NC * HALF, 2 * HID), pair)
        term[o] = part.reshape(NY, NC, HALF, 128)
        sb[o] = term[o, :, 1 - c].astype(BF16)
        rs[o] = send(sb.at[o], sr.at[o], rss.at[o], rsr.at[o], sibling)
    rx = []
    for o in (2, 1, 3):
        rs[o].wait_recv()
        xb[o] = (term[o, :, c] + sr[o].astype(F32)).astype(BF16)
        rx.append(send(xb.at[o], xr.at[o], rxs.at[o], rxr.at[o], device(z, xpeer(o), y, c)))

    for copy in cz:
        copy.wait_recv()
    held = cmr[...].reshape(TOKENS, 128)
    wt_hi, wt_lo = split2(corner_weights(held.astype(F32), FEAT, TOKENS))
    from_cot = (dot(held, wt_hi, TN) + dot(held, wt_lo, TN))[:FEAT]
    tau = iota((CAP, TOKENS), 1)
    rank = NZ * (tau & (BAL - 1)) + (tau >> 6)
    here = iota((CAP, TOKENS), 0)
    pick = jnp.where((rank - off == here) & (here < own_rows), 1.0, 0.0).astype(BF16)
    live_cot = jnp.where(iota((CAP, FEAT), 0) < own_rows, cot_ref[...].astype(F32), 0.0)

    rs[0].wait_recv()
    total = term[0, :, c] + sr[0].astype(F32)
    for copy in rx:
        copy.wait_recv()
    own_ref[...] = total + ((xr[1].astype(F32) + xr[3].astype(F32)) + xr[2].astype(F32))
    ry = []
    for o in (4, 3, 5, 2, 6, 1, 7):
        yb[o] = own_ref[ypeer(o)].astype(BF16)
        ry.append(send(yb.at[o], yr.at[o], rys.at[o], ryr.at[o], device(z, x, ypeer(o), c)))
    for copy in ry:
        copy.wait_recv()
    branch = own_ref[y]
    for o in range(1, NY):
        branch = branch + yr[o].astype(F32)
    gb[...] = branch.astype(BF16)
    gz = [
        send(gb, gr.at[z], gzs.at[o], gzr.at[o], device(zpeer(o), x, y, c)) for o in z_order
    ]
    gr[z] = gb[...]
    for copy in gz:
        copy.wait_recv()

    first = iota((HALF, 128), 1) < BAL
    tiles = []
    for e in range(0, NZ, 2):
        g0, g1 = gr[e].astype(F32), gr[e + 1].astype(F32)
        top = jnp.where(first, g0, pltpu.roll(g1, BAL, 1))
        bottom = jnp.where(first, pltpu.roll(g0, BAL, 1), g1)
        tiles.append(jnp.concatenate([top, bottom], axis=0).astype(BF16))
    grads = jnp.concatenate(tiles, axis=1)
    gp_ref[...] = live_cot + dot(pick, grads, NT)
    gt_ref[...] = from_cot + (dot(grads, wt_hi) + dot(grads, wt_lo))

    for copy in sent:
        copy.wait_send()


def shards(patches, table, row_anchor, row_frac, group_rows, up_weight, down_weight, cotangent):
    vmem = pl.BlockSpec(memory_space=pltpu.VMEM)
    hbm = pl.BlockSpec(memory_space=pl.ANY)
    sems = lambda n: pltpu.SemaphoreType.DMA((n,))
    grad_patches, grad_table = pl.pallas_call(
        kernel,
        name="branch_grad",
        out_shape=(
            jax.ShapeDtypeStruct((CAP, FEAT), F32),
            jax.ShapeDtypeStruct((FEAT, CELLS), F32),
        ),
        in_specs=[pl.BlockSpec(memory_space=pltpu.SMEM)] + [vmem] * 5 + [hbm] * 2,
        out_specs=(vmem, vmem),
        scratch_shapes=[
            pltpu.VMEM((D, HID), BF16),
            pltpu.VMEM((HID, D), BF16),
            pltpu.VMEM((NZ, PACK, 256), BF16),
            pltpu.VMEM((NZ, PACK, 256), BF16),
            pltpu.VMEM((BAL, 128), BF16),
            pltpu.VMEM((NZ, BAL, 128), BF16),
            pltpu.VMEM((NX, NY, NC, FEAT, 128), BF16),
            pltpu.VMEM((NX, NY, NC, HALF, 128), F32),
            pltpu.VMEM((NX, NY, HALF, 128), BF16),
            pltpu.VMEM((NX, NY, HALF, 128), BF16),
            pltpu.VMEM((NX, NY, HALF, 128), BF16),
            pltpu.VMEM((NX, NY, HALF, 128), BF16),
            pltpu.VMEM((NY, HALF, 128), BF16),
            pltpu.VMEM((NY, HALF, 128), BF16),
            pltpu.VMEM((HALF, 128), BF16),
            pltpu.VMEM((NZ, HALF, 128), BF16),
            pltpu.VMEM((NY, HALF, 128), F32),
            sems(2),
            sems(NZ), sems(NZ), sems(NZ), sems(NZ),
            sems(NY), sems(NY), sems(NX), sems(NX),
            sems(NX), sems(NX), sems(NX), sems(NX),
            sems(NX), sems(NX), sems(NY), sems(NY),
            sems(NZ), sems(NZ),
        ],
        compiler_params=pltpu.CompilerParams(
            collective_id=0, has_side_effects=True, vmem_limit_bytes=48 * 2**20
        ),
    )(
        group_rows, patches, cotangent, table.T, row_anchor.T, row_frac.T, up_weight, down_weight
    )
    return grad_patches, grad_table.T


def solution(mesh):
    in_specs = (
        P("dp", "mp"),
        P(None, "mp"),
        P("dp", None),
        P("dp", None),
        P(),
        P(None, "mp"),
        P("mp", None),
        P("dp", "mp"),
    )
    out_specs = (P("dp", "mp"), P(None, "mp"))
    return jax.shard_map(shards, mesh=mesh, in_specs=in_specs, out_specs=out_specs, check_vma=False)
```

time: 494 us -> 76.7 us (0.16); the launches traced: 487 us -> 76.3 us
  waiting for transfers between devices: 446 us -> 0 us
  Pallas kernels: 0 us -> 67.5 us
  matrix products: 18.1 us -> 0 us
  between operations: 13.9 us -> 0.66 us
    all_gather x2 -> x0, waiting for transfers between devices: 184 us -> none  [the longest x1 96.9 us: branch_grad(): in_piece = lax.all_gather(rows_in, 'mp', axis=1, tiled=True)]
    unnamed x5 -> x0, waiting for transfers between devices: 155 us -> none
    psum x1 -> x0, waiting for transfers between devices: 108 us -> none  [shards(): grad_table = lax.psum(partial_table, 'dp')]
    pallas_call x0 -> x1, Pallas kernels: none -> 67.5 us  [shards(): pl.pallas_call(kernel, name='branch_grad', out_shape=(jax.ShapeDtypeStruc...]
    unnamed x1 -> x0, matrix products: 11.2 us -> none
    dot_general x3 -> x0, matrix products: 6.88 us -> none  [the longest x1 4.72 us: branch_grad(): pre_sum = jnp.dot(in_piece, up_weight, preferred_element_type=jnp.float32)]
  transfers between devices with their start and end apart: 4 -> 0, of which waited for: 4 -> 0; matrix products, arithmetic and copies ran while one was open for 2% -> 0% of each run, Pallas kernels for 0% -> 0%
where the time goes in v1:
time: 76.7 us; the launch traced here: 76.3 us
  Pallas kernels  67.5 us (88%)
  local copies, waits for them, and re-layouts  8.12 us (11%)
    pallas_call x1, Pallas kernels, shards(): pl.pallas_call(kernel, name='branch_grad', out_shape=(jax.ShapeDtypeStruc...  67.5 us
    unnamed x16, local copies, waits for them, and re-layouts  8.12 us

profile of v1, /device:TPU:1, one launch (start us, length us, event | category | flops | bytes accessed | tf_op | source)
XLA Modules:
  0.0 76.3 jit_solution(16467030374618737549)
XLA Ops:
  0.6 0.0 copy-start
  0.6 2.3 %copy-done = bf16[6144,384]{1,0:T(8,128)(2,1)S(1)} copy-done((bf16[6144,384]{1,0:T(8,128)(2,1)S(1)}, bf16[6144,384]{1,0:T(8,128)(2,1)}, u32[]{:S(2)}) %copy-start) | copy-done | bytes 4718616
  3.0 0.0 copy-start.1
  3.0 0.9 %copy-done.1 = f32[256,96]{0,1:T(8,128)S(1)} copy-done((f32[256,96]{0,1:T(8,128)S(1)}, f32[256,96]{0,1:T(8,128)}, u32[]{:S(2)}) %copy-start.1) | copy-done | bytes 98328
  3.9 0.0 copy-start.2
  3.9 0.8 %copy-done.2 = bf16[192,96]{1,0:T(8,128)(2,1)S(1)} copy-done((bf16[192,96]{1,0:T(8,128)(2,1)S(1)}, bf16[192,96]{1,0:T(8,128)(2,1)}, u32[]{:S(2)}) %copy-start.2) | copy-done | bytes 36888
  4.7 0.0 copy-start.3
  4.7 0.8 %copy-done.3 = bf16[192,96]{1,0:T(8,128)(2,1)S(1)} copy-done((bf16[192,96]{1,0:T(8,128)(2,1)S(1)}, bf16[192,96]{1,0:T(8,128)(2,1)}, u32[]{:S(2)}) %copy-start.3) | copy-done | bytes 36888
  5.5 0.0 copy-start.4
  5.5 0.7 copy-done.4
  6.1 0.0 copy-start.5
  6.1 0.7 copy-done.5
  6.8 0.0 copy-start.6
  6.8 0.7 copy-done.6
  7.5 67.5 %branch_grad.1 = (f32[192,96]{1,0:T(8,128)S(1)}, f32[96,256]{1,0:T(8,128)S(1)}) custom-call(s32[12]{0:T(128)S(1)} %copy-done.6, bf16[192,96]{1,0:T(8,128)(2,1)S(1)} %copy-done.2, bf16[192,96]{1,0:T(8,128)(2,1)S(1)} %copy-done.3, f32[96,256]{1,0:T(8,128)S(1)} %bitcast.4, s32[2,192]{1,0:T(2,128)S(1)} %bitcast.6, f32[2,192]{1,0:T(2,128)S(1)} %bitcast.7, ...), custom_call_target="tpu_custom_call" | custom-call | tf_op jit(solution)/shard_map/branch_grad/pallas_call | solution.py:264
  75.0 0.6 copy.12
  75.7 0.6 copy.13
Async XLA Ops:
  0.6 2.3 %copy-start = (bf16[6144,384]{1,0:T(8,128)(2,1)S(1)}, bf16[6144,384]{1,0:T(8,128)(2,1)}, u32[]{:S(2)}) copy-start(bf16[6144,384]{1,0:T(8,128)(2,1)} %up_hbm.1) | copy-start | bytes 14155780
  3.0 0.9 %copy-start.1 = (f32[256,96]{0,1:T(8,128)S(1)}, f32[256,96]{0,1:T(8,128)}, u32[]{:S(2)}) copy-start(f32[256,96]{0,1:T(8,128)} %param.9) | copy-start | bytes 294916
  3.9 0.8 %copy-start.2 = (bf16[192,96]{1,0:T(8,128)(2,1)S(1)}, bf16[192,96]{1,0:T(8,128)(2,1)}, u32[]{:S(2)}) copy-start(bf16[192,96]{1,0:T(8,128)(2,1)} %patches_ref.1) | copy-start | bytes 110596
  4.7 0.8 %copy-start.3 = (bf16[192,96]{1,0:T(8,128)(2,1)S(1)}, bf16[192,96]{1,0:T(8,128)(2,1)}, u32[]{:S(2)}) copy-start(bf16[192,96]{1,0:T(8,128)(2,1)} %cot_ref.1) | copy-start | bytes 110596
  5.5 0.7 copy-start.4
  6.1 0.7 copy-start.5
  6.8 0.7 copy-start.6

commit v2 on v1

--- a/solution.py
+++ b/solution.py
@@ -14,7 +14,8 @@
 FEAT, HID = D // NMP, FF // NMP
 PACK = CAP // NZ
 HALF = FEAT // 2
-BLOCK = NY * NC * FEAT
+BLOCK = NX * 2 * NC * FEAT
+Y_ORDER = (1, 7, 6, 3, 2, 5, 4)
 NN = (((1,), (0,)), ((), ()))
 NT = (((1,), (1,)), ((), ()))
 TN = (((0,), (0,)), ((), ()))
@@ -51,10 +52,10 @@
 
 
 def kernel(
-    rows_ref, patches_ref, cot_ref, table_ref, anchor_ref, frac_ref, up_hbm, down_hbm,
+    rows_hbm, patches_hbm, cot_hbm, table_hbm, anchor_hbm, frac_hbm, up_hbm, down_hbm,
     gp_ref, gt_ref,
-    up, down, msg, zin, cm, cmr, xt, term, sb, sr, xb, xr, yb, yr, gb, gr, own_ref,
-    wsem, zs, zr, cs, cr, gys, gyr, gxs, gxr, gss, gsr, rss, rsr, rxs, rxr, rys, ryr, gzs, gzr,
+    rows_ref, patches_ref, cot_ref, table_ref, anchor_ref, frac_ref, up, down, msg, zin, cm, cmr, xt, up_sib, mine, theirs, xb, xr, yb, yr, gb, gr, own_ref,
+    wsem, zs, zr, cs, cr, gys, gyr, gxs, gxr, gss, gsr, uss, usr, ggs, ggr, rxs, rxr, rys, ryr, gzs, gzr,
 ):
     z, i = lax.axis_index("dp"), lax.axis_index("mp")
     x, y, c = i // (NY * NC), (i // NC) % NY, i % NC
@@ -64,7 +65,8 @@
 
     zpeer = lambda o: lax.rem(z + o, NZ)
     xpeer = lambda o: lax.rem(x + o, NX)
-    ypeer = lambda o: lax.rem(y + o, NY)
+    flip = lambda bit, m: lax.rem(lax.rem(y // bit, 2) + (m // bit) % 2, 2) * bit
+    ypeer = lambda m: flip(4, m) + flip(2, m) + flip(1, m)
     sibling = device(z, x, y, 1 - c)
     sent = []
 
@@ -76,17 +78,24 @@
         sent.append(copy)
         return copy
 
-    load_up = pltpu.make_async_copy(up_hbm, up, wsem.at[0])
-    load_down = pltpu.make_async_copy(down_hbm, down, wsem.at[1])
-    load_up.start()
-    load_down.start()
-
     barrier = pltpu.get_barrier_semaphore()
     peers = [device(zpeer(o), x, y, c) for o in (6, 5, 7, 4, 8, 3, 9, 2, 10, 1, 11)]
-    peers += [device(z, x, ypeer(o), c) for o in (4, 3, 5, 2, 6, 1, 7)]
+    peers += [device(z, x, ypeer(m), c) for m in Y_ORDER]
     peers += [device(z, xpeer(o), y, c) for o in (2, 1, 3)] + [sibling]
     for dev in peers:
         pl.semaphore_signal(barrier, inc=1, device_id=dev, device_id_type=MESH)
+
+    loads = [
+        pltpu.make_async_copy(src, dst, wsem.at[k])
+        for k, (src, dst) in enumerate((
+            (rows_hbm, rows_ref), (anchor_hbm, anchor_ref), (frac_hbm, frac_ref), (patches_hbm, patches_ref),
+            (table_hbm, table_ref), (cot_hbm, cot_ref), (up_hbm, up), (down_hbm, down),
+        ))
+    ]
+    for load in loads:
+        load.start()
+    for load in loads[:6]:
+        load.wait()
 
     starts, count = [], jnp.int32(0)
     for g in range(NZ):
@@ -134,6 +143,7 @@
         for o in z_order
     ]
     zin[z] = msg[z]
+    us = send(up_hbm.at[:, :, 1 - c], up_sib, uss.at[0], usr.at[0], sibling)
 
     lane = iota((1, CAP), 1)
     group, j = lane >> 4, lane & (PACK - 1)
@@ -152,62 +162,86 @@
     both = jnp.concatenate([rows[:, :128], rows[:, 128:]], axis=0)
     xt[x, y, c] = both.T[:FEAT].astype(BF16)
 
-    gy = [
-        send(xt.at[x, y, c], xt.at[x, y, c], gys.at[o], gyr.at[o], device(z, x, ypeer(o), c))
-        for o in (4, 3, 5, 2, 6, 1, 7)
-    ]
+    def chunk(m):
+        return xt.at[x, ypeer(m), c]
+
+    def to_x(m):
+        return [
+            send(chunk(m), chunk(m), gxs.at[o, m], gxr.at[o, m], device(z, xpeer(o), y, c))
+            for o in (2, 1, 3)
+        ]
+
+    def to_sibling(m):
+        line = xt.at[:, ypeer(m), c]
+        return send(line, line, gss.at[m], gsr.at[m], sibling)
+
+    gy = {
+        m: send(chunk(0), chunk(0), gys.at[m], gyr.at[m], device(z, x, ypeer(m), c))
+        for m in Y_ORDER
+    }
+    gx = {0: to_x(0)}
     cm[...] = rows[:, 128:].astype(BF16)
     cmr[z] = cm[...]
-    for copy in gy:
-        copy.wait_recv()
-    gx = {
-        o: send(xt.at[x, :, c], xt.at[x, :, c], gxs.at[o], gxr.at[o], device(z, xpeer(o), y, c))
-        for o in (2, 1, 3)
-    }
-    gs = {0: send(xt.at[x, :, c], xt.at[x, :, c], gss.at[0], gsr.at[0], sibling)}
     cz = [
         send(cm, cmr.at[z], cs.at[o], cr.at[o], device(zpeer(o), x, y, c)) for o in z_order
     ]
-
-    load_up.wait()
-    load_down.wait()
-
-    def products(b):
-        block = xt[b].reshape(BLOCK, 128)
-        at = pl.multiple_of(b * BLOCK, BLOCK)
-        return dot(block, up[pl.ds(at, BLOCK), :], TN), dot(down[:, pl.ds(at, BLOCK)], block)
-
-    gs[0].wait_recv()
-    pre, back = products(x)
-    for o in (1, 3, 2):
-        gx[o].wait_recv()
-        b = xpeer(NX - o)
-        gs[o] = send(xt.at[b, :, c], xt.at[b, :, c], gss.at[o], gsr.at[o], sibling)
-    for o in (1, 3, 2):
-        gs[o].wait_recv()
-        more = products(xpeer(NX - o))
-        pre, back = pre + more[0], back + more[1]
+    for m in Y_ORDER:
+        gy[m].wait_recv()
+        gx[m] = to_x(m)
+    for load in loads[6:]:
+        load.wait()
+
+    def products(m):
+        pair = ypeer(m) // 2
+        block = xt[:, pl.ds(2 * pair, 2)].reshape(BLOCK, 128)
+        weights = up[:, pl.ds(2 * pair, 2)].reshape(BLOCK, HID)
+        width = BLOCK // NX
+        columns = [
+            down[:, pl.ds(pl.multiple_of(xx * (D // NX) + pair * width, 128), width)]
+            for xx in range(NX)
+        ]
+        return dot(block, weights, TN), dot(jnp.concatenate(columns, axis=1), block)
+
+    gs, pre, back = {}, None, None
+
+    def add_products(m):
+        nonlocal pre, back
+        gs[m].wait_recv()
+        gs[m + 1].wait_recv()
+        more = products(m)
+        pre, back = more if pre is None else (pre + more[0], back + more[1])
+
+    done = []
+    for m in (0,) + Y_ORDER:
+        for copy in gx[m]:
+            copy.wait_recv()
+        gs[m] = to_sibling(m)
+        done.append(m)
+        if len(done) % 2 == 1 and len(done) > 1:
+            add_products(min(done[-3:-1]))
+    add_products(min(done[-2:]))
 
     low = iota((HID, 128), 1) < BAL
     grad = pltpu.roll(back, BAL, 1) * gelu_slope(pre.T)
     grad = jnp.where(low, grad, 0.0)
+    mine[...] = grad.astype(BF16)
+    gg = send(mine, theirs, ggs.at[0], ggr.at[0], sibling)
     pair = jnp.concatenate([grad, pltpu.roll(grad, BAL, 1)], axis=0).astype(BF16)
 
-    rs = {}
-    for o in (2, 1, 3, 0):
-        b = xpeer(o)
-        weights = up[pl.ds(pl.multiple_of(b * BLOCK, BLOCK), BLOCK), :]
-        weights = weights.reshape(NY * NC, 2, HALF, HID)
+    def terms(weights, grads):
         weights = jnp.concatenate([weights[:, 0], weights[:, 1]], axis=2)
-        part = dot(weights.reshape(NY * NC * HALF, 2 * HID), pair)
-        term[o] = part.reshape(NY, NC, HALF, 128)
-        sb[o] = term[o, :, 1 - c].astype(BF16)
-        rs[o] = send(sb.at[o], sr.at[o], rss.at[o], rsr.at[o], sibling)
+        return dot(weights.reshape(NY * HALF, 2 * HID), grads).reshape(NY, HALF, 128)
+
+    own_part = {o: terms(up[xpeer(o), :, c], pair) for o in (2, 1, 3, 0)}
+    us.wait_recv()
+    gg.wait_recv()
+    grad = theirs[...].astype(F32)
+    pair = jnp.concatenate([grad, pltpu.roll(grad, BAL, 1)], axis=0).astype(BF16)
     rx = []
     for o in (2, 1, 3):
-        rs[o].wait_recv()
-        xb[o] = (term[o, :, c] + sr[o].astype(F32)).astype(BF16)
+        xb[o] = (own_part[o] + terms(up_sib[xpeer(o)], pair)).astype(BF16)
         rx.append(send(xb.at[o], xr.at[o], rxs.at[o], rxr.at[o], device(z, xpeer(o), y, c)))
+    total = own_part[0] + terms(up_sib[x], pair)
 
     for copy in cz:
         copy.wait_recv()
@@ -220,15 +254,13 @@
     pick = jnp.where((rank - off == here) & (here < own_rows), 1.0, 0.0).astype(BF16)
     live_cot = jnp.where(iota((CAP, FEAT), 0) < own_rows, cot_ref[...].astype(F32), 0.0)
 
-    rs[0].wait_recv()
-    total = term[0, :, c] + sr[0].astype(F32)
     for copy in rx:
         copy.wait_recv()
     own_ref[...] = total + ((xr[1].astype(F32) + xr[3].astype(F32)) + xr[2].astype(F32))
     ry = []
-    for o in (4, 3, 5, 2, 6, 1, 7):
-        yb[o] = own_ref[ypeer(o)].astype(BF16)
-        ry.append(send(yb.at[o], yr.at[o], rys.at[o], ryr.at[o], device(z, x, ypeer(o), c)))
+    for m in reversed(Y_ORDER):
+        yb[m] = own_ref[ypeer(m)].astype(BF16)
+        ry.append(send(yb.at[m], yr.at[m], rys.at[m], ryr.at[m], device(z, x, ypeer(m), c)))
     for copy in ry:
         copy.wait_recv()
     branch = own_ref[y]
@@ -257,10 +289,15 @@
         copy.wait_send()
 
 
+def copy_out(a_ref, b_ref, a_out, b_out):
+    a_out[...] = a_ref[...]
+    b_out[...] = b_ref[...]
+
+
 def shards(patches, table, row_anchor, row_frac, group_rows, up_weight, down_weight, cotangent):
     vmem = pl.BlockSpec(memory_space=pltpu.VMEM)
-    hbm = pl.BlockSpec(memory_space=pl.ANY)
-    sems = lambda n: pltpu.SemaphoreType.DMA((n,))
+    hbm = pl.BlockSpec(memory_space=pltpu.HBM)
+    sems = lambda *n: pltpu.SemaphoreType.DMA(n)
     grad_patches, grad_table = pl.pallas_call(
         kernel,
         name="branch_grad",
@@ -268,19 +305,25 @@
             jax.ShapeDtypeStruct((CAP, FEAT), F32),
             jax.ShapeDtypeStruct((FEAT, CELLS), F32),
         ),
-        in_specs=[pl.BlockSpec(memory_space=pltpu.SMEM)] + [vmem] * 5 + [hbm] * 2,
+        in_specs=[hbm] * 8,
         out_specs=(vmem, vmem),
         scratch_shapes=[
-            pltpu.VMEM((D, HID), BF16),
+            pltpu.SMEM((NZ,), jnp.int32),
+            pltpu.VMEM((CAP, FEAT), BF16),
+            pltpu.VMEM((CAP, FEAT), BF16),
+            pltpu.VMEM((FEAT, CELLS), F32),
+            pltpu.VMEM((2, CAP), jnp.int32),
+            pltpu.VMEM((2, CAP), F32),
+            pltpu.VMEM((NX, NY, NC, 2, HALF, HID), BF16),
             pltpu.VMEM((HID, D), BF16),
             pltpu.VMEM((NZ, PACK, 256), BF16),
             pltpu.VMEM((NZ, PACK, 256), BF16),
             pltpu.VMEM((BAL, 128), BF16),
             pltpu.VMEM((NZ, BAL, 128), BF16),
             pltpu.VMEM((NX, NY, NC, FEAT, 128), BF16),
-            pltpu.VMEM((NX, NY, NC, HALF, 128), F32),
-            pltpu.VMEM((NX, NY, HALF, 128), BF16),
-            pltpu.VMEM((NX, NY, HALF, 128), BF16),
+            pltpu.VMEM((NX, NY, 2, HALF, HID), BF16),
+            pltpu.VMEM((HID, 128), BF16),
+            pltpu.VMEM((HID, 128), BF16),
             pltpu.VMEM((NX, NY, HALF, 128), BF16),
             pltpu.VMEM((NX, NY, HALF, 128), BF16),
             pltpu.VMEM((NY, HALF, 128), BF16),
@@ -288,19 +331,29 @@
             pltpu.VMEM((HALF, 128), BF16),
             pltpu.VMEM((NZ, HALF, 128), BF16),
             pltpu.VMEM((NY, HALF, 128), F32),
-            sems(2),
+            sems(8),
             sems(NZ), sems(NZ), sems(NZ), sems(NZ),
-            sems(NY), sems(NY), sems(NX), sems(NX),
-            sems(NX), sems(NX), sems(NX), sems(NX),
+            sems(NY), sems(NY), sems(NX, NY), sems(NX, NY), sems(NY), sems(NY), sems(1), sems(1), sems(1), sems(1),
             sems(NX), sems(NX), sems(NY), sems(NY),
             sems(NZ), sems(NZ),
         ],
         compiler_params=pltpu.CompilerParams(
-            collective_id=0, has_side_effects=True, vmem_limit_bytes=48 * 2**20
+            collective_id=0, has_side_effects=True, vmem_limit_bytes=60 * 2**20
         ),
     )(
-        group_rows, patches, cotangent, table.T, row_anchor.T, row_frac.T, up_weight, down_weight
+        group_rows, patches, cotangent, table.T, row_anchor.T, row_frac.T,
+        up_weight.reshape(NX, NY, NC, 2, HALF, HID), down_weight,
     )
+    grad_patches, grad_table = pl.pallas_call(
+        copy_out,
+        name="copy_out",
+        out_shape=(
+            jax.ShapeDtypeStruct((CAP, FEAT), F32),
+            jax.ShapeDtypeStruct((FEAT, CELLS), F32),
+        ),
+        in_specs=[vmem] * 2,
+        out_specs=(vmem, vmem),
+    )(grad_patches, grad_table)
     return grad_patches, grad_table.T
 
 

time: 76.7 us -> 67.7 us (0.88)
  local copies, waits for them, and re-layouts: 8.12 us -> 0 us
    unnamed x16 -> x0, local copies, waits for them, and re-layouts: 8.12 us -> none
    pallas_call x1, Pallas kernels: 67.5 us -> 65.3 us  [shards(): pl.pallas_call(kernel, name='branch_grad', out_shape=(jax.ShapeDtypeStruc...]
    pallas_call x0 -> x1, Pallas kernels: none -> 1.62 us  [shards(): pl.pallas_call(copy_out, name='copy_out', out_shape=(jax.ShapeDtypeStruct...]
where the time goes in v2:
time: 67.7 us; the launch traced here: 67.5 us
  Pallas kernels  66.9 us (99%)
    pallas_call x1, Pallas kernels, shards(): pl.pallas_call(kernel, name='branch_grad', out_shape=(jax.ShapeDtypeStruc...  65.3 us
    pallas_call x1, Pallas kernels, shards(): pl.pallas_call(copy_out, name='copy_out', out_shape=(jax.ShapeDtypeStruct...  1.62 us

profile of v2, /device:TPU:1, one launch (start us, length us, event | category | flops | bytes accessed | tf_op | source)
XLA Modules:
  0.0 67.5 jit_solution(96433751211746229)
XLA Ops:
  0.6 65.3 %branch_grad.1 = (f32[192,96]{1,0:T(8,128)}, f32[96,256]{1,0:T(8,128)}) custom-call(s32[12]{0:T(128)} %rows_hbm.1, bf16[192,96]{1,0:T(8,128)(2,1)} %patches_hbm.1, bf16[192,96]{1,0:T(8,128)(2,1)} %cot_hbm.1, f32[96,256]{1,0:T(8,128)} %bitcast.6, s32[2,192]{1,0:T(2,128)} %bitcast.7, f32[2,192]{1,0:T(2,128)} %bitcast.8, ...), custom_call_target="tpu_custom_call" | custom-call | tf_op jit(solution)/shard_map/branch_grad/pallas_call | solution.py:301
  65.9 1.6 %copy_out.1 = (f32[192,96]{1,0:T(8,128)}, f32[96,256]{1,0:T(8,128)}) custom-call(f32[192,96]{1,0:T(8,128)} %get-tuple-element.6.a_ref, f32[96,256]{1,0:T(8,128)} %get-tuple-element.7.b_ref), custom_call_target="tpu_custom_call" | custom-call | tf_op jit(solution)/shard_map/copy_out/pallas_call | solution.py:347

commit v3 on v2

--- a/solution.py
+++ b/solution.py
@@ -15,7 +15,8 @@
 PACK = CAP // NZ
 HALF = FEAT // 2
 BLOCK = NX * 2 * NC * FEAT
-Y_ORDER = (1, 7, 6, 3, 2, 5, 4)
+Y_ORDER = (1, 7, 2, 6, 3, 5, 4)
+STREAMS = ((0, 16), (16, 32))
 NN = (((1,), (0,)), ((), ()))
 NT = (((1,), (1,)), ((), ()))
 TN = (((0,), (0,)), ((), ()))
@@ -65,8 +66,7 @@
 
     zpeer = lambda o: lax.rem(z + o, NZ)
     xpeer = lambda o: lax.rem(x + o, NX)
-    flip = lambda bit, m: lax.rem(lax.rem(y // bit, 2) + (m // bit) % 2, 2) * bit
-    ypeer = lambda m: flip(4, m) + flip(2, m) + flip(1, m)
+    ypeer = lambda o: lax.rem(y + o, NY)
     sibling = device(z, x, y, 1 - c)
     sent = []
 
@@ -163,7 +163,7 @@
     xt[x, y, c] = both.T[:FEAT].astype(BF16)
 
     def chunk(m):
-        return xt.at[x, ypeer(m), c]
+        return xt.at[x, ypeer(NY - m), c]
 
     def to_x(m):
         return [
@@ -172,7 +172,7 @@
         ]
 
     def to_sibling(m):
-        line = xt.at[:, ypeer(m), c]
+        line = xt.at[:, ypeer(NY - m), c]
         return send(line, line, gss.at[m], gsr.at[m], sibling)
 
     gy = {
@@ -191,8 +191,7 @@
     for load in loads[6:]:
         load.wait()
 
-    def products(m):
-        pair = ypeer(m) // 2
+    def products(pair):
         block = xt[:, pl.ds(2 * pair, 2)].reshape(BLOCK, 128)
         weights = up[:, pl.ds(2 * pair, 2)].reshape(BLOCK, HID)
         width = BLOCK // NX
@@ -202,24 +201,21 @@
         ]
         return dot(block, weights, TN), dot(jnp.concatenate(columns, axis=1), block)
 
-    gs, pre, back = {}, None, None
-
-    def add_products(m):
-        nonlocal pre, back
-        gs[m].wait_recv()
-        gs[m + 1].wait_recv()
-        more = products(m)
-        pre, back = more if pre is None else (pre + more[0], back + more[1])
-
-    done = []
-    for m in (0,) + Y_ORDER:
+    half, odd = y // 2, lax.rem(y, 2)
+    turns = (0, 3 - 2 * odd, 1 + 2 * odd, 2)
+    gs, pre, back, whole = {}, None, None, []
+    arrivals = (0,) + Y_ORDER
+    for n, m in enumerate(arrivals):
         for copy in gx[m]:
             copy.wait_recv()
         gs[m] = to_sibling(m)
-        done.append(m)
-        if len(done) % 2 == 1 and len(done) > 1:
-            add_products(min(done[-3:-1]))
-    add_products(min(done[-2:]))
+        for t in {3: (0,), 5: (1,), 7: (2, 3)}.get(n, ()):
+            for k in arrivals[: (3, 5, 7, 8)[t]]:
+                if k not in whole:
+                    gs[k].wait_recv()
+                    whole.append(k)
+            more = products(lax.rem(half + turns[t], NY // 2))
+            pre, back = more if pre is None else (pre + more[0], back + more[1])
 
     low = iota((HID, 128), 1) < BAL
     grad = pltpu.roll(back, BAL, 1) * gelu_slope(pre.T)
@@ -228,48 +224,68 @@
     gg = send(mine, theirs, ggs.at[0], ggr.at[0], sibling)
     pair = jnp.concatenate([grad, pltpu.roll(grad, BAL, 1)], axis=0).astype(BF16)
 
-    def terms(weights, grads):
+    def terms(weights, grads, first, n):
+        weights = weights[:, :, first : first + n]
         weights = jnp.concatenate([weights[:, 0], weights[:, 1]], axis=2)
-        return dot(weights.reshape(NY * HALF, 2 * HID), grads).reshape(NY, HALF, 128)
-
-    own_part = {o: terms(up[xpeer(o), :, c], pair) for o in (2, 1, 3, 0)}
+        return dot(weights.reshape(NY * n, 2 * HID), grads).reshape(NY, n, 128)
+
+    own_part = {
+        (h, o): terms(up[xpeer(o), :, c], pair, *rows)
+        for h, rows in enumerate(STREAMS)
+        for o in (2, 1, 3, 0)
+    }
     us.wait_recv()
     gg.wait_recv()
     grad = theirs[...].astype(F32)
     pair = jnp.concatenate([grad, pltpu.roll(grad, BAL, 1)], axis=0).astype(BF16)
-    rx = []
-    for o in (2, 1, 3):
-        xb[o] = (own_part[o] + terms(up_sib[xpeer(o)], pair)).astype(BF16)
-        rx.append(send(xb.at[o], xr.at[o], rxs.at[o], rxr.at[o], device(z, xpeer(o), y, c)))
-    total = own_part[0] + terms(up_sib[x], pair)
+    rx = {}
+    for h, (first, n) in enumerate(STREAMS):
+        at = pl.ds(first, n)
+        for o in (2, 1, 3):
+            part = own_part[h, o] + terms(up_sib[xpeer(o)], pair, first, n)
+            xb[o, :, at] = part.astype(BF16)
+            rx[h, o] = send(
+                xb.at[o, :, at], xr.at[o, :, at], rxs.at[h, o], rxr.at[h, o], device(z, xpeer(o), y, c)
+            )
+    for h, (first, n) in enumerate(STREAMS):
+        own_ref[:, pl.ds(first, n)] = own_part[h, 0] + terms(up_sib[x], pair, first, n)
 
     for copy in cz:
         copy.wait_recv()
     held = cmr[...].reshape(TOKENS, 128)
     wt_hi, wt_lo = split2(corner_weights(held.astype(F32), FEAT, TOKENS))
     from_cot = (dot(held, wt_hi, TN) + dot(held, wt_lo, TN))[:FEAT]
+
+    ry = {}
+    for h, (first, n) in enumerate(STREAMS):
+        at = pl.ds(first, n)
+        for o in (2, 1, 3):
+            rx[h, o].wait_recv()
+        total = xr[1, :, at].astype(F32) + xr[3, :, at].astype(F32)
+        own_ref[:, at] = own_ref[:, at] + (total + xr[2, :, at].astype(F32))
+        for m in reversed(Y_ORDER):
+            yb[m, at] = own_ref[ypeer(m), at].astype(BF16)
+            ry[h, m] = send(
+                yb.at[m, at], yr.at[m, at], rys.at[h, m], ryr.at[h, m], device(z, x, ypeer(m), c)
+            )
     tau = iota((CAP, TOKENS), 1)
     rank = NZ * (tau & (BAL - 1)) + (tau >> 6)
     here = iota((CAP, TOKENS), 0)
     pick = jnp.where((rank - off == here) & (here < own_rows), 1.0, 0.0).astype(BF16)
     live_cot = jnp.where(iota((CAP, FEAT), 0) < own_rows, cot_ref[...].astype(F32), 0.0)
-
-    for copy in rx:
-        copy.wait_recv()
-    own_ref[...] = total + ((xr[1].astype(F32) + xr[3].astype(F32)) + xr[2].astype(F32))
-    ry = []
-    for m in reversed(Y_ORDER):
-        yb[m] = own_ref[ypeer(m)].astype(BF16)
-        ry.append(send(yb.at[m], yr.at[m], rys.at[m], ryr.at[m], device(z, x, ypeer(m), c)))
-    for copy in ry:
-        copy.wait_recv()
-    branch = own_ref[y]
-    for o in range(1, NY):
-        branch = branch + yr[o].astype(F32)
-    gb[...] = branch.astype(BF16)
-    gz = [
-        send(gb, gr.at[z], gzs.at[o], gzr.at[o], device(zpeer(o), x, y, c)) for o in z_order
-    ]
+    gz = []
+    for h, (first, n) in enumerate(STREAMS):
+        at = pl.ds(first, n)
+        for m in Y_ORDER:
+            ry[h, m].wait_recv()
+        branch = own_ref[y, at]
+        for m in range(1, NY):
+            branch = branch + yr[m, at].astype(F32)
+        gb[at] = branch.astype(BF16)
+        gz += [
+            send(gb.at[at], gr.at[z, at], gzs.at[h, o], gzr.at[h, o], device(zpeer(o), x, y, c))
+            for o in z_order
+        ]
     gr[z] = gb[...]
     for copy in gz:
         copy.wait_recv()
@@ -334,8 +350,8 @@
             sems(8),
             sems(NZ), sems(NZ), sems(NZ), sems(NZ),
             sems(NY), sems(NY), sems(NX, NY), sems(NX, NY), sems(NY), sems(NY), sems(1), sems(1), sems(1), sems(1),
-            sems(NX), sems(NX), sems(NY), sems(NY),
-            sems(NZ), sems(NZ),
+            sems(2, NX), sems(2, NX), sems(2, NY), sems(2, NY),
+            sems(2, NZ), sems(2, NZ),
         ],
         compiler_params=pltpu.CompilerParams(
             collective_id=0, has_side_effects=True, vmem_limit_bytes=60 * 2**20

time: 67.7 us -> 65.7 us (0.970)
  Pallas kernels: 66.9 us -> 64.9 us
    pallas_call x1, Pallas kernels: 65.3 us -> 63.3 us  [shards(): pl.pallas_call(kernel, name='branch_grad', out_shape=(jax.ShapeDtypeStruc...]
where the time goes in v3:
time: 65.7 us; the launch traced here: 65.5 us
  Pallas kernels  64.9 us (99%)
    pallas_call x1, Pallas kernels, shards(): pl.pallas_call(kernel, name='branch_grad', out_shape=(jax.ShapeDtypeStruc...  63.3 us
    pallas_call x1, Pallas kernels, shards(): pl.pallas_call(copy_out, name='copy_out', out_shape=(jax.ShapeDtypeStruct...  1.62 us

profile of v3, /device:TPU:1, one launch (start us, length us, event | category | flops | bytes accessed | tf_op | source)
XLA Modules:
  0.0 65.5 jit_solution(9443271802230066661)
XLA Ops:
  0.6 63.3 %branch_grad.1 = (f32[192,96]{1,0:T(8,128)}, f32[96,256]{1,0:T(8,128)}) custom-call(s32[12]{0:T(128)} %rows_hbm.1, bf16[192,96]{1,0:T(8,128)(2,1)} %patches_hbm.1, bf16[192,96]{1,0:T(8,128)(2,1)} %cot_hbm.1, f32[96,256]{1,0:T(8,128)} %bitcast.6, s32[2,192]{1,0:T(2,128)} %bitcast.7, f32[2,192]{1,0:T(2,128)} %bitcast.8, ...), custom_call_target="tpu_custom_call" | custom-call | tf_op jit(solution)/shard_map/branch_grad/pallas_call | solution.py:317
  63.9 1.6 %copy_out.1 = (f32[192,96]{1,0:T(8,128)}, f32[96,256]{1,0:T(8,128)}) custom-call(f32[192,96]{1,0:T(8,128)} %get-tuple-element.6.a_ref, f32[96,256]{1,0:T(8,128)} %get-tuple-element.7.b_ref), custom_call_target="tpu_custom_call" | custom-call | tf_op jit(solution)/shard_map/copy_out/pallas_call | solution.py:363

commit v4 on v3

--- a/solution.py
+++ b/solution.py
@@ -15,8 +15,9 @@
 PACK = CAP // NZ
 HALF = FEAT // 2
 BLOCK = NX * 2 * NC * FEAT
-Y_ORDER = (1, 7, 2, 6, 3, 5, 4)
-STREAMS = ((0, 16), (16, 32))
+Y_ORDER = (1, 7, 4, 3, 5, 2, 6)
+Y_FAR = (4, 5, 3, 6, 2, 7, 1)
+STREAMS = ((0, 16), (16, 16), (32, 16))
 NN = (((1,), (0,)), ((), ()))
 NT = (((1,), (1,)), ((), ()))
 TN = (((0,), (0,)), ((), ()))
@@ -201,16 +202,15 @@
         ]
         return dot(block, weights, TN), dot(jnp.concatenate(columns, axis=1), block)
 
-    half, odd = y // 2, lax.rem(y, 2)
-    turns = (0, 3 - 2 * odd, 1 + 2 * odd, 2)
+    half, turns = y // 2, (0, 2, 3, 1)
     gs, pre, back, whole = {}, None, None, []
     arrivals = (0,) + Y_ORDER
     for n, m in enumerate(arrivals):
         for copy in gx[m]:
             copy.wait_recv()
         gs[m] = to_sibling(m)
-        for t in {3: (0,), 5: (1,), 7: (2, 3)}.get(n, ()):
-            for k in arrivals[: (3, 5, 7, 8)[t]]:
+        for t in {3: (0,), 6: (1,), 7: (2, 3)}.get(n, ()):
+            for k in arrivals[: (3, 6, 7, 8)[t]]:
                 if k not in whole:
                     gs[k].wait_recv()
                     whole.append(k)
@@ -263,7 +263,7 @@
             rx[h, o].wait_recv()
         total = xr[1, :, at].astype(F32) + xr[3, :, at].astype(F32)
         own_ref[:, at] = own_ref[:, at] + (total + xr[2, :, at].astype(F32))
-        for m in reversed(Y_ORDER):
+        for m in Y_FAR:
             yb[m, at] = own_ref[ypeer(m), at].astype(BF16)
             ry[h, m] = send(
                 yb.at[m, at], yr.at[m, at], rys.at[h, m], ryr.at[h, m], device(z, x, ypeer(m), c)
@@ -287,6 +287,8 @@
             for o in z_order
         ]
     gr[z] = gb[...]
+    for copy in sent:
+        copy.wait_send()
     for copy in gz:
         copy.wait_recv()
 
@@ -300,9 +302,6 @@
     grads = jnp.concatenate(tiles, axis=1)
     gp_ref[...] = live_cot + dot(pick, grads, NT)
     gt_ref[...] = from_cot + (dot(grads, wt_hi) + dot(grads, wt_lo))
-
-    for copy in sent:
-        copy.wait_send()
 
 
 def copy_out(a_ref, b_ref, a_out, b_out):
@@ -350,8 +349,8 @@
             sems(8),
             sems(NZ), sems(NZ), sems(NZ), sems(NZ),
             sems(NY), sems(NY), sems(NX, NY), sems(NX, NY), sems(NY), sems(NY), sems(1), sems(1), sems(1), sems(1),
-            sems(2, NX), sems(2, NX), sems(2, NY), sems(2, NY),
-            sems(2, NZ), sems(2, NZ),
+            sems(3, NX), sems(3, NX), sems(3, NY), sems(3, NY),
+            sems(3, NZ), sems(3, NZ),
         ],
         compiler_params=pltpu.CompilerParams(
             collective_id=0, has_side_effects=True, vmem_limit_bytes=60 * 2**20

time: 65.7 us -> 65.2 us (level); the launches traced: 65.5 us -> 64.1 us
  Pallas kernels: 64.9 us -> 63.5 us
    pallas_call x1, Pallas kernels: 63.3 us -> 61.9 us  [shards(): pl.pallas_call(kernel, name='branch_grad', out_shape=(jax.ShapeDtypeStruc...]
where the time goes in v4:
time: 65.2 us; the launch traced here: 64.1 us
  Pallas kernels  63.5 us (97%)
    pallas_call x1, Pallas kernels, shards(): pl.pallas_call(kernel, name='branch_grad', out_shape=(jax.ShapeDtypeStruc...  61.9 us
    pallas_call x1, Pallas kernels, shards(): pl.pallas_call(copy_out, name='copy_out', out_shape=(jax.ShapeDtypeStruct...  1.62 us

profile of v4, /device:TPU:1, one launch (start us, length us, event | category | flops | bytes accessed | tf_op | source)
XLA Modules:
  0.0 64.1 jit_solution(4309691232268454740)
XLA Ops:
  0.6 61.9 %branch_grad.1 = (f32[192,96]{1,0:T(8,128)}, f32[96,256]{1,0:T(8,128)}) custom-call(s32[12]{0:T(128)} %rows_hbm.1, bf16[192,96]{1,0:T(8,128)(2,1)} %patches_hbm.1, bf16[192,96]{1,0:T(8,128)(2,1)} %cot_hbm.1, f32[96,256]{1,0:T(8,128)} %bitcast.6, s32[2,192]{1,0:T(2,128)} %bitcast.7, f32[2,192]{1,0:T(2,128)} %bitcast.8, ...), custom_call_target="tpu_custom_call" | custom-call | tf_op jit(solution)/shard_map/branch_grad/pallas_call | solution.py:316
  62.5 1.6 %copy_out.1 = (f32[192,96]{1,0:T(8,128)}, f32[96,256]{1,0:T(8,128)}) custom-call(f32[192,96]{1,0:T(8,128)} %get-tuple-element.6.a_ref, f32[96,256]{1,0:T(8,128)} %get-tuple-element.7.b_ref), custom_call_target="tpu_custom_call" | custom-call | tf_op jit(solution)/shard_map/copy_out/pallas_call | solution.py:362

commit v5 on v4

--- a/solution.py
+++ b/solution.py
@@ -183,12 +183,12 @@
     gx = {0: to_x(0)}
     cm[...] = rows[:, 128:].astype(BF16)
     cmr[z] = cm[...]
+    for m in Y_ORDER:
+        gy[m].wait_recv()
+        gx[m] = to_x(m)
     cz = [
         send(cm, cmr.at[z], cs.at[o], cr.at[o], device(zpeer(o), x, y, c)) for o in z_order
     ]
-    for m in Y_ORDER:
-        gy[m].wait_recv()
-        gx[m] = to_x(m)
     for load in loads[6:]:
         load.wait()
 

time: 65.2 us -> 65.2 us (level)
  no operation moved by 1% of the time
where the time goes in v5:
time: 65.2 us; the launch traced here: 64.1 us
  Pallas kernels  63.5 us (97%)
    pallas_call x1, Pallas kernels, shards(): pl.pallas_call(kernel, name='branch_grad', out_shape=(jax.ShapeDtypeStruc...  61.9 us
    pallas_call x1, Pallas kernels, shards(): pl.pallas_call(copy_out, name='copy_out', out_shape=(jax.ShapeDtypeStruct...  1.62 us

profile of v5, /device:TPU:1, one launch (start us, length us, event | category | flops | bytes accessed | tf_op | source)
XLA Modules:
  0.0 64.1 jit_solution(16520902923476791953)
XLA Ops:
  0.6 61.9 %branch_grad.1 = (f32[192,96]{1,0:T(8,128)}, f32[96,256]{1,0:T(8,128)}) custom-call(s32[12]{0:T(128)} %rows_hbm.1, bf16[192,96]{1,0:T(8,128)(2,1)} %patches_hbm.1, bf16[192,96]{1,0:T(8,128)(2,1)} %cot_hbm.1, f32[96,256]{1,0:T(8,128)} %bitcast.6, s32[2,192]{1,0:T(2,128)} %bitcast.7, f32[2,192]{1,0:T(2,128)} %bitcast.8, ...), custom_call_target="tpu_custom_call" | custom-call | tf_op jit(solution)/shard_map/branch_grad/pallas_call | solution.py:316
  62.5 1.6 %copy_out.1 = (f32[192,96]{1,0:T(8,128)}, f32[96,256]{1,0:T(8,128)}) custom-call(f32[192,96]{1,0:T(8,128)} %get-tuple-element.6.a_ref, f32[96,256]{1,0:T(8,128)} %get-tuple-element.7.b_ref), custom_call_target="tpu_custom_call" | custom-call | tf_op jit(solution)/shard_map/copy_out/pallas_call | solution.py:362
